TPU v7x, 32 devices: a whole 2x2x4 slice. The times are simulated.
32 devices in a mesh: gx: 8 (over y, x, core), gy: 4 (over z).
Axes of the slice: x: 2, y: 2, z: 4, core: 2. Of those that a mesh axis runs over, the one named last changes fastest.
Arguments:
- positions: float32 [3, 32, 16, 256], P(None, 'gx', 'gy'), may hold values from 0 to 1
- velocity: float32 [3, 32, 16, 256], P(None, 'gx', 'gy'), may hold values from -3 to 3
- density: float32 [32, 16, 256], P('gx', 'gy'), may hold values from 0.7 to 1.3
- cell_fill: int32 [32, 16], P('gx', 'gy'), may hold values from 64 to 256
- pair_cells: int32 [8, 4, 2, 86], P('gx', 'gy'), may hold values from 0 to 35, as said below
- pair_counts: int32 [8, 4, 2], P('gx', 'gy'), may hold values from 0 to 86, as said below
- shell_nodes: int32 [4, 32, 16], P(None, 'gx', 'gy'), may hold values from 0 to 32767, as said below
- shell_weights: float32 [4, 32, 16], P(None, 'gx', 'gy'), may hold values from 0.2 to 1
- shell_links: int32 [4, 32768], P(None, 'gx'), may hold values from 0 to 4095
- shell_disp: float32 [3, 32768], P(None, 'gx'), may hold values from -3 to 3
- shell_vel: float32 [3, 32768], P(None, 'gx'), may hold values from -3 to 3
Outputs:
- fluid_velocity: float32 [3, 32, 16, 256], P(None, 'gx', 'gy')
- fluid_density: float32 [32, 16, 256], P('gx', 'gy')
- shell_speed: float32 [3, 32768], P(None, 'gx')
- shell_offset: float32 [3, 32768], P(None, 'gx')
Inputs may be any that keep to these rules, and one draw needn't show every extreme that they name: pair_cells[i, j, 0, s] and pair_cells[i, j, 1, s] are row-major flat indices into the (6) x (6) block of device (i, j) extended by one cell on each side; below pair_counts[i, j, 1] they name two distinct neighbouring cells (8-neighbourhood), the first inside the block, the second inside the grid, no unordered pair twice; a pair inside one block is listed by that device only, below pair_counts[i, j, 0]; a pair of cells on two devices is listed by both, below pair_counts[.., 0] on exactly one of them. pair_counts[i, j, 0] <= pair_counts[i, j, 1]. `shell_nodes`: a cell in cell columns x * 4 to (x + 1) * 4 - 1 is tied only to nodes of strips x - 1, x and x + 1, strip x holding nodes x * 4096 to (x + 1) * 4096 - 1.
All inputs are finite; a program needn't handle non-finite values.
Results may differ from a plain program's by a relative error of at most 0.0001.
Values sent between devices are 32-bit elements; how exact they have to be, the bound alone decides.
A program may use at most 64 MiB of HBM per device.

v0:
```python
import jax
import jax.numpy as jnp
from jax import lax
from jax.sharding import PartitionSpec as P

SUBSTEPS = 2


stiffness = 2.0
viscosity = 0.5
particle_mass = 0.02
time_step = 0.5
contact_depth = 0.5
wall_stiffness = 0.1
wall_drag = 0.2
shell_compliance = 0.2
shell_spring = 0.5
tile_group = 4


def with_halo(shard, sides, width):
    for axis, dim in sides:
        peers, length = (lax.axis_size(axis), shard.shape[dim])
        up = [(i, (i + 1) % peers) for i in range(peers - 1)]
        down = [(j, i) for i, j in up]
        last = lax.slice_in_dim(shard, length - width, length, axis=dim)
        first = lax.slice_in_dim(shard, 0, width, axis=dim)
        before = lax.ppermute(last, axis, up)
        after = lax.ppermute(first, axis, down)
        shard = jnp.concatenate([before, shard, after], axis=dim)
    return shard


def tile_fields(geo_a, geo_b, fluid_a, fluid_b, shift_x, shift_y):
    gap_x = (geo_a[0] + shift_x)[:, None] - geo_b[0][None, :]
    gap_y = (geo_a[1] + shift_y)[:, None] - geo_b[1][None, :]
    gap_z = geo_a[2][:, None] - geo_b[2][None, :]
    closeness = jnp.maximum(1.0 - (gap_x * gap_x + gap_y * gap_y + gap_z * gap_z), 0.0)
    weight = closeness * closeness * (geo_a[3][:, None] * geo_b[3][None, :])
    press_a = stiffness * (fluid_a[3] - 1.0)
    press_b = stiffness * (fluid_b[3] - 1.0)
    thrust = (press_a[:, None] + press_b[None, :]) * weight
    diff_x = fluid_a[0][:, None] - fluid_b[0][None, :]
    diff_y = fluid_a[1][:, None] - fluid_b[1][None, :]
    diff_z = fluid_a[2][:, None] - fluid_b[2][None, :]
    force_x = thrust * gap_x - viscosity * weight * diff_x
    force_y = thrust * gap_y - viscosity * weight * diff_y
    force_z = thrust * gap_z - viscosity * weight * diff_z
    density_rate = weight * (diff_x * gap_x + diff_y * gap_y + diff_z * gap_z)
    return (force_x, force_y, force_z, density_rate)


def self_terms(geo_a, fluid_a):
    fields = tile_fields(geo_a, geo_a, fluid_a, fluid_a, 0.0, 0.0)
    return jnp.stack(
        [jnp.sum(fields[0], 1), jnp.sum(fields[1], 1), jnp.sum(fields[2], 1), jnp.sum(fields[3], 1)]
    )


def pair_terms(geo_a, geo_b, fluid_a, fluid_b, shift_x, shift_y):
    fields = tile_fields(geo_a, geo_b, fluid_a, fluid_b, shift_x, shift_y)
    row_sums = jnp.stack(
        [jnp.sum(fields[0], 1), jnp.sum(fields[1], 1), jnp.sum(fields[2], 1), jnp.sum(fields[3], 1)]
    )
    col_sums = jnp.stack(
        [
            -jnp.sum(fields[0], 0),
            -jnp.sum(fields[1], 0),
            -jnp.sum(fields[2], 0),
            jnp.sum(fields[3], 0),
        ]
    )
    return (row_sums, col_sums)


def wall_force(positions, velocity, live_mask, coupled):
    contact = jnp.maximum(1.0 - positions[2] / contact_depth, 0.0)
    contact = contact * contact * live_mask
    drag = wall_drag * contact * (coupled[..., None] - velocity)
    return drag.at[2].add(wall_stiffness * contact)


def shell_update(disp, shell_speed, node_force, links):
    beside_all = jnp.sum(disp[:, links], 1)
    spring_force = links.shape[0] * disp - beside_all
    new_speed = shell_speed + time_step * (
        shell_compliance * node_force - shell_spring * spring_force
    )
    return (new_speed, disp + time_step * new_speed)


def run_self(gathered, geo_own, fluid_own, interior):

    def self_turn(turn_index, sums):
        picked = turn_index * tile_group + jnp.arange(tile_group, dtype=jnp.int32)
        row_sums = jax.vmap(self_terms, in_axes=(0, 0), out_axes=0)(
            geo_own[picked], fluid_own[picked]
        )
        return sums.at[interior[picked]].add(row_sums)

    return lax.fori_loop(0, interior.shape[0] // tile_group, self_turn, gathered)


def run_pairs(gathered, count, pair_list, geo_pad, fluid_pad, ny_pad):

    def pair_turn(turn_index, sums):
        picked = turn_index * tile_group + jnp.arange(tile_group, dtype=jnp.int32)
        valid = (picked < count).astype(jnp.float32)
        picked = jnp.minimum(picked, pair_list.shape[1] - 1)
        first = pair_list[0][picked]
        second = pair_list[1][picked]
        shift_x = (first // ny_pad - second // ny_pad).astype(jnp.float32)
        shift_y = (first % ny_pad - second % ny_pad).astype(jnp.float32)
        row_sums, col_sums = jax.vmap(pair_terms, in_axes=(0, 0, 0, 0, 0, 0), out_axes=0)(
            geo_pad[first], geo_pad[second], fluid_pad[first], fluid_pad[second], shift_x, shift_y
        )
        sums = sums.at[first].add(row_sums * valid[:, None, None])
        return sums.at[second].add(col_sums * valid[:, None, None])

    turns = (count + tile_group - 1) // tile_group
    return lax.fori_loop(0, turns, pair_turn, gathered)


def return_partials(full, returned):
    interior = full[1:-1, 1:-1]
    interior = interior.at[0, :].add(returned[0, 2:-2])
    interior = interior.at[-1, :].add(returned[-1, 2:-2])
    interior = interior.at[:, 0].add(returned[2:-2, 0])
    interior = interior.at[:, -1].add(returned[2:-2, -1])
    interior = interior.at[0, 0].add(returned[0, 0])
    interior = interior.at[0, -1].add(returned[0, -1])
    interior = interior.at[-1, 0].add(returned[-1, 0])
    return interior.at[-1, -1].add(returned[-1, -1])


def body(
    positions,
    velocity,
    density,
    cell_fill,
    pair_cells,
    pair_counts,
    shell_nodes,
    shell_weights,
    shell_links,
    shell_disp,
    shell_vel,
):
    rows_x, rows_y, particles = density.shape
    ny_pad = rows_y + 2
    pad_cells = (rows_x + 2) * ny_pad
    strip_len = shell_vel.shape[1]
    column = lax.axis_index("gx")
    slot_iota = lax.broadcasted_iota(jnp.int32, density.shape, 2)
    live_mask = (slot_iota < cell_fill[:, :, None]).astype(jnp.float32)
    geometry = jnp.concatenate([jnp.moveaxis(positions, 0, 2), live_mask[:, :, None]], 2)
    geo_pad = with_halo(geometry, (("gx", 0), ("gy", 1)), 1).reshape(pad_cells, 4, particles)
    geo_own = geometry.reshape(rows_x * rows_y, 4, particles)
    interior = (
        (jnp.arange(rows_x, dtype=jnp.int32)[:, None] + 1) * ny_pad
        + jnp.arange(rows_y, dtype=jnp.int32)[None, :]
        + 1
    ).reshape(-1)
    pair_list = pair_cells[0, 0]
    totals = pair_counts[0, 0]
    local_ids = shell_nodes - (column - 1) * strip_len
    for substep in range(SUBSTEPS):
        fluid = jnp.concatenate([jnp.moveaxis(velocity, 0, 2), density[:, :, None]], 2)
        fluid_own = fluid.reshape(rows_x * rows_y, 4, particles)
        sums = run_self(
            jnp.zeros((pad_cells, 4, particles), jnp.float32), geo_own, fluid_own, interior
        )
        fluid_pad = with_halo(fluid, (("gx", 0), ("gy", 1)), 1).reshape(pad_cells, 4, particles)
        sums = run_pairs(sums, totals[0], pair_list, geo_pad, fluid_pad, ny_pad)
        full = sums.reshape(rows_x + 2, rows_y + 2, 4, particles)
        returned = with_halo(full, (("gx", 0), ("gy", 1)), 1)
        cell_forces = return_partials(full, returned)
        forces = jnp.moveaxis(cell_forces, 2, 0)
        window = with_halo(shell_vel, (("gx", 1),), strip_len)
        coupled = jnp.sum(window[:, local_ids] * shell_weights[None], 1)
        wall_push = wall_force(positions, velocity, live_mask, coupled)
        wall_load = -jnp.sum(wall_push, 3)
        shares = shell_weights[None] * wall_load[:, None]
        nearby = jnp.zeros((3, 3 * strip_len), jnp.float32).at[:, local_ids].add(shares)
        received = with_halo(nearby, (("gx", 1),), strip_len)
        strip_part = (
            nearby[:, strip_len : 2 * strip_len]
            + received[:, 0:strip_len]
            + received[:, 4 * strip_len : 5 * strip_len]
        )
        node_force = lax.psum(strip_part, "gy")
        shell_vel, shell_disp = shell_update(shell_disp, shell_vel, node_force, shell_links)
        velocity = velocity + time_step * (particle_mass * forces[0:3] + wall_push)
        density = density + time_step * particle_mass * forces[3]
    return (velocity, density, shell_vel, shell_disp)


def solution(mesh):
    return jax.shard_map(
        body,
        mesh=mesh,
        in_specs=(
            P(None, "gx", "gy", None),
            P(None, "gx", "gy", None),
            P("gx", "gy", None),
            P("gx", "gy"),
            P("gx", "gy", None, None),
            P("gx", "gy", None),
            P(None, "gx", "gy"),
            P(None, "gx", "gy"),
            P(None, "gx"),
            P(None, "gx"),
            P(None, "gx"),
        ),
        out_specs=(P(None, "gx", "gy", None), P("gx", "gy", None), P(None, "gx"), P(None, "gx")),
        check_vma=False,
    )
```

profile of v0, /device:TPU:0, one launch (start us, length us, event | category | flops | bytes accessed | tf_op | source)
XLA Modules:
  0.0 616.2 jit_solution(8774359468617637403)
XLA Ops:
  7.2 5.1 collective-permute-start
  21.0 20.5 %while.78 = (s32[]{:T(128)}, f32[36,4,256]{2,1,0:T(4,128)S(1)}, f32[16,4,256]{2,1,0:T(4,128)S(1)}, f32[16,4,256]{2,1,0:T(4,128)S(1)}, s32[4]{0:T(128)S(1)}, /*index=5*/s32[]{:T(128)}, s32[]{:T(128)}) while((s32[]{:T(128)}, f32[36,4,256]{2,1,0:T(4,128)S(1)}, f32[16,4,256]{2,1,0:T(4,128)S(1)}, f32[16,4,256]{2,1,0:T(4,128)S(1)}, ...), condition=%wide.region_6.0_spmd.clone, body=%wide.region_0.0_spmd.clone.sunk | while | flops 9976895 | bytes 365013 | solution.py:101
  43.5 54.4 %gather_fusion.19 = f32[16384,3]{1,0:T(8,128)} fusion(f32[3,4096]{0,1:T(8,128)S(1)} %copy.259, s32[16384]{0:T(1024)S(1)} %broadcast_clamp_fusion), kind=kCustom, calls=%fused_computation.19 | custom fusion | bytes 458752 | tf_op jit(solution)/shard_map/gather | solution.py:84
  97.9 4.2 reduce.43
  102.8 4.4 collective-permute-start.4
  108.6 4.5 collective-permute-start.2
  114.5 4.5 collective-permute-start.6
  120.8 110.0 %while.76 = (s32[]{:T(128)}, f32[36,4,256]{2,1,0:T(4,128)S(1)}, s32[]{:T(128)}, s32[2,86]{1,0:T(2,128)S(1)}, f32[36,4,256]{2,1,0:T(4,128)S(1)}, /*index=5*/f32[3...) while((s32[]{:T(128)}, f32[36,4,256]{2,1,0:T(4,128)S(1)}, s32[]{:T(128)}, s32[2,86]{1,0:T(2,128)S(1)}, ...), condition=%wide.region_18.19_spmd, body=%wide.region_7.18_spmd.sunk | while | flops 11055275 | bytes 759709 | solution.py:121
  230.9 9.8 %collective-permute-start.8 = (f32[1,6,4,256]{3,1,0,2:T(8,128)S(1)}, f32[1,6,4,256]{3,1,0,2:T(8,128)S(1)}, u32[]{:S(2)}, u32[]{:S(2)}) collective-permute-start(f32[1,6,4,256]{3,1,0,2:T(8,128)S(1)} %get-tuple-element.1004), channel_id=1, source_target_pairs={{0,4},{4,8},{8,12},{12,16},{16,20},{20,24},{24,28},{1,5},{5,9},{9,... | collective-permute-start | bytes 73736 | tf_op jit(solution)/shard_map/ppermute | solution.py:28
  242.1 4.0 copy.244
  246.1 3.4 gather_fusion.18
  250.2 3.8 scatter_custom_fusion.6
  254.0 5.3 fusion.145
  265.7 14.3 %collective-permute-start.22 = (f32[3,4096]{1,0:T(4,128)S(1)}, f32[3,4096]{1,0:T(4,128)S(1)}, u32[]{:S(2)}, u32[]{:S(2)}) collective-permute-start(f32[3,4096]{1,0:T(4,128)S(1)} %copy.257), channel_id=1, source_target_pairs={{0,4},{4,8},{8,12},{12,16},{16,20},{20,24},{24,28},{1,5},{5,9},{9,... | collective-permute-start | bytes 147464 | tf_op jit(solution)/shard_map/ppermute | solution.py:28
  280.2 12.1 %collective-permute-start.10 = (f32[8,1,4,256]{3,1,0,2:T(1,128)S(1)}, f32[8,1,4,256]{3,1,0,2:T(1,128)S(1)}, u32[]{:S(2)}, u32[]{:S(2)}) collective-permute-start(f32[8,1,4,256]{3,1,0,2:T(1,128)S(1)} %copy.321), channel_id=1, source_target_pairs={{0,1},{1,2},{2,3},{4,5},{5,6},{6,7},{8,9},{9,10},{10,11},{12,13},{... | collective-permute-start | bytes 98312 | tf_op jit(solution)/shard_map/ppermute | solution.py:28
  293.9 4.1 collective-permute-done.11
  301.8 16.5 %psum.14 = f32[3,4096]{1,0:T(4,128)S(1)} all-reduce(f32[3,4096]{1,0:T(4,128)S(1)} %add_add_fusion.3), channel_id=1, replica_groups=mesh['gx'=8,'gy'=4] {'gy'}, use_global_device_ids=true, to_apply=%region_42.43 | all-reduce | flops 12288 | bytes 98304 | tf_op jit(solution)/shard_map/psum | solution.py:191
  323.6 54.4 %gather_fusion.21 = f32[16384,3]{1,0:T(8,128)} fusion(f32[3,4096]{0,1:T(8,128)S(1)} %copy.267, s32[16384]{0:T(1024)S(1)} %broadcast_clamp_fusion), kind=kCustom, calls=%fused_computation.21 | custom fusion | bytes 458752 | tf_op jit(solution)/shard_map/gather | solution.py:84
  378.0 4.2 reduce.44
  382.9 4.0 copy.261
  391.9 4.8 collective-permute-start.14
  398.9 4.5 collective-permute-start.16
  403.5 20.5 %while.79 = (s32[]{:T(128)}, f32[36,4,256]{2,1,0:T(4,128)S(1)}, f32[16,4,256]{2,1,0:T(4,128)S(1)}, f32[16,4,256]{2,1,0:T(4,128)S(1)}, s32[4]{0:T(128)S(1)}, /*index=5*/s32[]{:T(128)}, s32[]{:T(128)}) while((s32[]{:T(128)}, f32[36,4,256]{2,1,0:T(4,128)S(1)}, f32[16,4,256]{2,1,0:T(4,128)S(1)}, f32[16,4,256]{2,1,0:T(4,128)S(1)}, ...), condition=%wide.region_27.28_spmd.clone, body=%wide.region_21.27_spmd.clone.sunk | while | flops 9976895 | bytes 365013 | solution.py:101
  424.2 110.0 %while.77 = (s32[]{:T(128)}, f32[36,4,256]{2,1,0:T(4,128)S(1)}, s32[]{:T(128)}, s32[2,86]{1,0:T(2,128)S(1)}, f32[36,4,256]{2,1,0:T(4,128)S(1)}, /*index=5*/f32[3...) while((s32[]{:T(128)}, f32[36,4,256]{2,1,0:T(4,128)S(1)}, s32[]{:T(128)}, s32[2,86]{1,0:T(2,128)S(1)}, ...), condition=%wide.region_39.40_spmd, body=%wide.region_28.39_spmd.sunk | while | flops 11055275 | bytes 759709 | solution.py:121
  534.3 11.0 %collective-permute-start.18 = (f32[1,6,4,256]{3,1,0,2:T(8,128)S(1)}, f32[1,6,4,256]{3,1,0,2:T(8,128)S(1)}, u32[]{:S(2)}, u32[]{:S(2)}) collective-permute-start(f32[1,6,4,256]{3,1,0,2:T(8,128)S(1)} %get-tuple-element.1002), channel_id=1, source_target_pairs={{0,4},{4,8},{8,12},{12,16},{16,20},{20,24},{24,28},{1,5},{5,9},{9,... | collective-permute-start | bytes 73736 | tf_op jit(solution)/shard_map/ppermute | solution.py:28
  546.7 11.9 %collective-permute-done.19 = f32[1,6,4,256]{3,1,0,2:T(8,128)S(1)} collective-permute-done((f32[1,6,4,256]{3,1,0,2:T(8,128)S(1)}, f32[1,6,4,256]{3,1,0,2:T(8,128)S(1)}, u32[]{:S(2)}, u32[]{:S(2)}) %collective-permute-start.19) | collective-permute-done | bytes 24608 | tf_op jit(solution)/shard_map/ppermute | solution.py:29
  558.7 9.8 %collective-permute-start.20 = (f32[8,1,4,256]{3,1,0,2:T(1,128)S(1)}, f32[8,1,4,256]{3,1,0,2:T(1,128)S(1)}, u32[]{:S(2)}, u32[]{:S(2)}) collective-permute-start(f32[8,1,4,256]{3,1,0,2:T(1,128)S(1)} %get-tuple-element.998), channel_id=1, source_target_pairs={{0,1},{1,2},{2,3},{4,5},{5,6},{6,7},{8,9},{9,10},{10,11},{12,13},{... | collective-permute-start | bytes 98312 | tf_op jit(solution)/shard_map/ppermute | solution.py:28
  570.2 4.1 collective-permute-done.21
  578.8 3.8 scatter_custom_fusion.7
  582.7 5.3 fusion.144
  593.7 3.7 collective-permute-start.26
  598.7 16.8 %psum.15 = f32[3,4096]{1,0:T(4,128)S(1)} all-reduce(f32[3,4096]{1,0:T(4,128)S(1)} %add_add_fusion.2), channel_id=1, replica_groups=mesh['gx'=8,'gy'=4] {'gy'}, use_global_device_ids=true, to_apply=%region_47.48 | all-reduce | flops 12288 | bytes 98304 | tf_op jit(solution)/shard_map/psum | solution.py:191
  (1331 shorter events, 319.8 us)
Async XLA Ops:
  0.6 41.4 %copy-start.8 = (s32[4]{0:T(128)S(1)}, s32[4]{0:T(128)}, u32[]{:S(2)}) copy-start(s32[4]{0:T(128)} %constant.854.clone.1) | copy-start | bytes 52
  0.6 42.1 %copy-start.9 = (s32[1,1,2]{2,1,0:T(1,128)S(1)}, s32[1,1,2]{2,1,0:T(1,128)}, u32[]{:S(2)}) copy-start(s32[1,1,2]{2,1,0:T(1,128)} %param.60) | copy-start | bytes 28
  0.7 42.2 %copy-start.3 = (f32[3,4096]{1,0:T(4,128)S(1)}, f32[3,4096]{1,0:T(4,128)}, u32[]{:S(2)}) copy-start(f32[3,4096]{1,0:T(4,128)} %param.64) | copy-start | bytes 147460
  0.7 241.4 %collective-permute-start.13 = (f32[3,4096]{1,0:T(4,128)}, f32[3,4096]{1,0:T(4,128)S(1)}, u32[]{:S(2)}, u32[]{:S(2)}) collective-permute-start(f32[3,4096]{1,0:T(4,128)} %param.65), channel_id=1, source_target_pairs={{4,0},{8,4},{12,8},{16,12},{20,16},{24,20},{28,24},{5,1},{9,5},{13... | collective-permute-start | bytes 147464 | tf_op jit(solution)/shard_map/ppermute | solution.py:29
  2.1 240.0 %collective-permute-start.12 = (f32[3,4096]{1,0:T(4,128)}, f32[3,4096]{1,0:T(4,128)S(1)}, u32[]{:S(2)}, u32[]{:S(2)}) collective-permute-start(f32[3,4096]{1,0:T(4,128)} %param.65), channel_id=1, source_target_pairs={{0,4},{4,8},{8,12},{12,16},{16,20},{20,24},{24,28},{1,5},{5,9},{9,... | collective-permute-start | bytes 147464 | tf_op jit(solution)/shard_map/ppermute | solution.py:28
  5.9 96.8 %collective-permute-start.1 = (f32[1,4,4,256]{3,1,0,2:T(4,128)S(1)}, f32[1,4,4,256]{3,1,0,2:T(4,128)S(1)}, u32[]{:S(2)}, u32[]{:S(2)}) collective-permute-start(f32[1,4,4,256]{3,1,0,2:T(4,128)S(1)} %get-tuple-element.1018), channel_id=1, source_target_pairs={{4,0},{8,4},{12,8},{16,12},{20,16},{24,20},{28,24},{5,1},{9,5},{13... | collective-permute-start | bytes 49160 | tf_op jit(solution)/shard_map/ppermute | solution.py:29
  7.2 100.0 %collective-permute-start = (f32[1,4,4,256]{3,1,0,2:T(4,128)S(1)}, f32[1,4,4,256]{3,1,0,2:T(4,128)S(1)}, u32[]{:S(2)}, u32[]{:S(2)}) collective-permute-start(f32[1,4,4,256]{3,1,0,2:T(4,128)S(1)} %get-tuple-element.1017), channel_id=1, source_target_pairs={{0,4},{4,8},{8,12},{12,16},{16,20},{20,24},{24,28},{1,5},{5,9},{9,... | collective-permute-start | bytes 49160 | tf_op jit(solution)/shard_map/ppermute | solution.py:28
  13.8 94.8 %collective-permute-start.5 = (f32[1,4,4,256]{3,1,0,2:T(4,128)S(1)}, f32[1,4,4,256]{3,1,0,2:T(4,128)S(1)}, u32[]{:S(2)}, u32[]{:S(2)}) collective-permute-start(f32[1,4,4,256]{3,1,0,2:T(4,128)S(1)} %get-tuple-element.1016), channel_id=1, source_target_pairs={{4,0},{8,4},{12,8},{16,12},{20,16},{24,20},{28,24},{5,1},{9,5},{13... | collective-permute-start | bytes 49160 | tf_op jit(solution)/shard_map/ppermute | solution.py:29
  102.7 139.3 %copy-start.4 = (f32[3,4096]{1,0:T(4,128)S(1)}, f32[3,4096]{1,0:T(4,128)}, u32[]{:S(2)}) copy-start(f32[3,4096]{1,0:T(4,128)} %param.65) | copy-start | bytes 147460
  102.8 10.4 %collective-permute-start.4 = (f32[1,4,4,256]{3,1,0,2:T(4,128)S(1)}, f32[1,4,4,256]{3,1,0,2:T(4,128)S(1)}, u32[]{:S(2)}, u32[]{:S(2)}) collective-permute-start(f32[1,4,4,256]{3,1,0,2:T(4,128)S(1)} %get-tuple-element.1015), channel_id=1, source_target_pairs={{0,4},{4,8},{8,12},{12,16},{16,20},{20,24},{24,28},{1,5},{5,9},{9,... | collective-permute-start | bytes 49160 | tf_op jit(solution)/shard_map/ppermute | solution.py:28
  107.2 7.2 %collective-permute-start.3 = (f32[6,1,4,256]{3,1,0,2:T(1,128)S(1)}, f32[6,1,4,256]{3,1,0,2:T(1,128)S(1)}, u32[]{:S(2)}, u32[]{:S(2)}) collective-permute-start(f32[6,1,4,256]{3,1,0,2:T(1,128)S(1)} %get-tuple-element.1012), channel_id=1, source_target_pairs={{1,0},{2,1},{3,2},{5,4},{6,5},{7,6},{9,8},{10,9},{11,10},{13,12},{... | collective-permute-start | bytes 73736 | tf_op jit(solution)/shard_map/ppermute | solution.py:29
  108.6 10.5 %collective-permute-start.2 = (f32[6,1,4,256]{3,1,0,2:T(1,128)S(1)}, f32[6,1,4,256]{3,1,0,2:T(1,128)S(1)}, u32[]{:S(2)}, u32[]{:S(2)}) collective-permute-start(f32[6,1,4,256]{3,1,0,2:T(1,128)S(1)} %get-tuple-element.1011), channel_id=1, source_target_pairs={{0,1},{1,2},{2,3},{4,5},{5,6},{6,7},{8,9},{9,10},{10,11},{12,13},{... | collective-permute-start | bytes 73736 | tf_op jit(solution)/shard_map/ppermute | solution.py:28
  113.2 6.1 collective-permute-start.7
  114.5 6.1 collective-permute-start.6
  230.9 49.1 %collective-permute-start.8 = (f32[1,6,4,256]{3,1,0,2:T(8,128)S(1)}, f32[1,6,4,256]{3,1,0,2:T(8,128)S(1)}, u32[]{:S(2)}, u32[]{:S(2)}) collective-permute-start(f32[1,6,4,256]{3,1,0,2:T(8,128)S(1)} %get-tuple-element.1004), channel_id=1, source_target_pairs={{0,4},{4,8},{8,12},{12,16},{16,20},{20,24},{24,28},{1,5},{5,9},{9,... | collective-permute-start | bytes 73736 | tf_op jit(solution)/shard_map/ppermute | solution.py:28
  240.7 39.3 %collective-permute-start.9 = (f32[1,6,4,256]{3,1,0,2:T(8,128)S(1)}, f32[1,6,4,256]{3,1,0,2:T(8,128)S(1)}, u32[]{:S(2)}, u32[]{:S(2)}) collective-permute-start(f32[1,6,4,256]{3,1,0,2:T(8,128)S(1)} %get-tuple-element.1003), channel_id=1, source_target_pairs={{4,0},{8,4},{12,8},{16,12},{20,16},{24,20},{28,24},{5,1},{9,5},{13... | collective-permute-start | bytes 73736 | tf_op jit(solution)/shard_map/ppermute | solution.py:29
  261.5 40.2 %collective-permute-start.23 = (f32[3,4096]{1,0:T(4,128)S(1)}, f32[3,4096]{1,0:T(4,128)S(1)}, u32[]{:S(2)}, u32[]{:S(2)}) collective-permute-start(f32[3,4096]{1,0:T(4,128)S(1)} %copy.258), channel_id=1, source_target_pairs={{4,0},{8,4},{12,8},{16,12},{20,16},{24,20},{28,24},{5,1},{9,5},{13... | collective-permute-start | bytes 147464 | tf_op jit(solution)/shard_map/ppermute | solution.py:29
  265.7 36.1 %collective-permute-start.22 = (f32[3,4096]{1,0:T(4,128)S(1)}, f32[3,4096]{1,0:T(4,128)S(1)}, u32[]{:S(2)}, u32[]{:S(2)}) collective-permute-start(f32[3,4096]{1,0:T(4,128)S(1)} %copy.257), channel_id=1, source_target_pairs={{0,4},{4,8},{8,12},{12,16},{16,20},{20,24},{24,28},{1,5},{5,9},{9,... | collective-permute-start | bytes 147464 | tf_op jit(solution)/shard_map/ppermute | solution.py:28
  280.2 13.7 %collective-permute-start.10 = (f32[8,1,4,256]{3,1,0,2:T(1,128)S(1)}, f32[8,1,4,256]{3,1,0,2:T(1,128)S(1)}, u32[]{:S(2)}, u32[]{:S(2)}) collective-permute-start(f32[8,1,4,256]{3,1,0,2:T(1,128)S(1)} %copy.321), channel_id=1, source_target_pairs={{0,1},{1,2},{2,3},{4,5},{5,6},{6,7},{8,9},{9,10},{10,11},{12,13},{... | collective-permute-start | bytes 98312 | tf_op jit(solution)/shard_map/ppermute | solution.py:28
  292.2 5.8 collective-permute-start.11
  318.4 64.5 %collective-permute-start.25 = (f32[3,4096]{1,0:T(4,128)S(1)}, f32[3,4096]{1,0:T(4,128)S(1)}, u32[]{:S(2)}, u32[]{:S(2)}) collective-permute-start(f32[3,4096]{1,0:T(4,128)S(1)} %get-tuple-element.880), channel_id=1, source_target_pairs={{4,0},{8,4},{12,8},{16,12},{20,16},{24,20},{28,24},{5,1},{9,5},{13... | collective-permute-start | bytes 147464 | tf_op jit(solution)/shard_map/ppermute | solution.py:29
  319.7 63.2 %collective-permute-start.24 = (f32[3,4096]{1,0:T(4,128)S(1)}, f32[3,4096]{1,0:T(4,128)S(1)}, u32[]{:S(2)}, u32[]{:S(2)}) collective-permute-start(f32[3,4096]{1,0:T(4,128)S(1)} %get-tuple-element.880), channel_id=1, source_target_pairs={{0,4},{4,8},{8,12},{12,16},{16,20},{20,24},{24,28},{1,5},{5,9},{9,... | collective-permute-start | bytes 147464 | tf_op jit(solution)/shard_map/ppermute | solution.py:28
  390.6 6.2 %collective-permute-start.15 = (f32[1,4,4,256]{3,1,0,2:T(4,128)S(1)}, f32[1,4,4,256]{3,1,0,2:T(4,128)S(1)}, u32[]{:S(2)}, u32[]{:S(2)}) collective-permute-start(f32[1,4,4,256]{3,1,0,2:T(4,128)S(1)} %get-tuple-element.1014), channel_id=1, source_target_pairs={{4,0},{8,4},{12,8},{16,12},{20,16},{24,20},{28,24},{5,1},{9,5},{13... | collective-permute-start | bytes 49160 | tf_op jit(solution)/shard_map/ppermute | solution.py:29
  391.9 5.7 collective-permute-start.14
  397.6 26.4 %collective-permute-start.17 = (f32[6,1,4,256]{3,1,0,2:T(1,128)S(1)}, f32[6,1,4,256]{3,1,0,2:T(1,128)S(1)}, u32[]{:S(2)}, u32[]{:S(2)}) collective-permute-start(f32[6,1,4,256]{3,1,0,2:T(1,128)S(1)} %get-tuple-element.1008), channel_id=1, source_target_pairs={{1,0},{2,1},{3,2},{5,4},{6,5},{7,6},{9,8},{10,9},{11,10},{13,12},{... | collective-permute-start | bytes 73736 | tf_op jit(solution)/shard_map/ppermute | solution.py:29
  398.9 25.1 %collective-permute-start.16 = (f32[6,1,4,256]{3,1,0,2:T(1,128)S(1)}, f32[6,1,4,256]{3,1,0,2:T(1,128)S(1)}, u32[]{:S(2)}, u32[]{:S(2)}) collective-permute-start(f32[6,1,4,256]{3,1,0,2:T(1,128)S(1)} %get-tuple-element.1007), channel_id=1, source_target_pairs={{0,1},{1,2},{2,3},{4,5},{5,6},{6,7},{8,9},{9,10},{10,11},{12,13},{... | collective-permute-start | bytes 73736 | tf_op jit(solution)/shard_map/ppermute | solution.py:28
  534.3 12.4 %collective-permute-start.18 = (f32[1,6,4,256]{3,1,0,2:T(8,128)S(1)}, f32[1,6,4,256]{3,1,0,2:T(8,128)S(1)}, u32[]{:S(2)}, u32[]{:S(2)}) collective-permute-start(f32[1,6,4,256]{3,1,0,2:T(8,128)S(1)} %get-tuple-element.1002), channel_id=1, source_target_pairs={{0,4},{4,8},{8,12},{12,16},{16,20},{20,24},{24,28},{1,5},{5,9},{9,... | collective-permute-start | bytes 73736 | tf_op jit(solution)/shard_map/ppermute | solution.py:28
  545.3 13.3 %collective-permute-start.19 = (f32[1,6,4,256]{3,1,0,2:T(8,128)S(1)}, f32[1,6,4,256]{3,1,0,2:T(8,128)S(1)}, u32[]{:S(2)}, u32[]{:S(2)}) collective-permute-start(f32[1,6,4,256]{3,1,0,2:T(8,128)S(1)} %get-tuple-element.1001), channel_id=1, source_target_pairs={{4,0},{8,4},{12,8},{16,12},{20,16},{24,20},{28,24},{5,1},{9,5},{13... | collective-permute-start | bytes 73736 | tf_op jit(solution)/shard_map/ppermute | solution.py:29
  558.7 11.4 %collective-permute-start.20 = (f32[8,1,4,256]{3,1,0,2:T(1,128)S(1)}, f32[8,1,4,256]{3,1,0,2:T(1,128)S(1)}, u32[]{:S(2)}, u32[]{:S(2)}) collective-permute-start(f32[8,1,4,256]{3,1,0,2:T(1,128)S(1)} %get-tuple-element.998), channel_id=1, source_target_pairs={{0,1},{1,2},{2,3},{4,5},{5,6},{6,7},{8,9},{9,10},{10,11},{12,13},{... | collective-permute-start | bytes 98312 | tf_op jit(solution)/shard_map/ppermute | solution.py:28
  568.5 5.8 collective-permute-start.21
  590.2 8.5 %collective-permute-start.27 = (f32[3,4096]{1,0:T(4,128)S(1)}, f32[3,4096]{1,0:T(4,128)S(1)}, u32[]{:S(2)}, u32[]{:S(2)}) collective-permute-start(f32[3,4096]{1,0:T(4,128)S(1)} %copy.266), channel_id=1, source_target_pairs={{4,0},{8,4},{12,8},{16,12},{20,16},{24,20},{28,24},{5,1},{9,5},{13... | collective-permute-start | bytes 147464 | tf_op jit(solution)/shard_map/ppermute | solution.py:29
  593.7 5.0 collective-permute-start.26
  (6 other events, 94.3 us)
where the time goes:
time: 621 us; the launch traced here: 616 us
  local copies, waits for them, and re-layouts  272 us (44%)
  other arithmetic  167 us (27%)
  starting transfers between devices  113 us (18%)
  blocking collectives  33.3 us (5%)
  waiting for transfers between devices  22.8 us (4%)
    gather x2, local copies, waits for them, and re-layouts, shell_update(): beside_all = jnp.sum(disp[:, links], 1)  109 us
    ppermute x14, starting transfers between devices, with_halo(): before = lax.ppermute(last, axis, up)  94.9 us
    reduce_sum x28, other arithmetic, pair_terms(): jnp.sum(fields[0], 0)  68.5 us
    psum x2, blocking collectives, body(): node_force = lax.psum(strip_part, 'gy')  33.3 us
    ppermute x14, waiting for transfers between devices, with_halo(): after = lax.ppermute(first, axis, down)  20.2 us
    reduce_sum x8, other arithmetic, self_terms(): jnp.sum(fields[0], 1)  18.8 us
    scatter-add x28, other arithmetic, pair_turn(): sums = sums.at[first].add(row_sums * valid[:, None, None])  18.3 us
    ppermute x14, starting transfers between devices, with_halo(): after = lax.ppermute(first, axis, down)  18.2 us
  transfers between devices with their start and end apart: 28, of which 7 were waited for; matrix products, arithmetic and copies ran while one was open for 50% of the time, Pallas kernels for 0%

commit v1 on v0

v1 whole, which is shorter than its diff:
```python
import functools

import jax
import jax.numpy as jnp
from jax import lax
from jax.experimental import pallas as pl
from jax.experimental.pallas import tpu as pltpu
from jax.sharding import PartitionSpec as P

F32 = jnp.float32
BF16 = jnp.bfloat16
MESH = pl.DeviceIdType.MESH
LANES = 128
DIRS = [(a, b) for a in (-1, 0, 1) for b in (-1, 0, 1)]


def iota(shape, dim):
    return lax.broadcasted_iota(jnp.int32, shape, dim)


def split3(value):
    high = value.astype(BF16).astype(F32)
    rest = value - high
    mid = rest.astype(BF16).astype(F32)
    low = (rest - mid).astype(BF16).astype(F32)
    return high, mid, low


def dot(a, b):
    return jnp.dot(a, b, preferred_element_type=F32)


def dot_t(a, b):
    return lax.dot_general(a, b, (((1,), (1,)), ((), ())), preferred_element_type=F32)


def table_of(rows):
    return jnp.concatenate(split3(rows), axis=1).astype(BF16)


def kernel(
    nx, ny,
    pos_ref, vel_ref, rho_ref, fill_ref, pairs_ref, counts_ref, ties_ref, links_ref, disp_ref, svel_ref,
    vel_out, rho_out, speed_out, offset_out,
    posS, velS, rhoS, liveS, pushS, forS, pad1, pad2, win1, win2, msg1, msg2,
    alive, dtab, dtable, beside, node, left, right, loads, whigh, wlow,
    halo_send, halo_recv, win_send, win_recv, msg_send, msg_recv,
):
    cxl, cyl, cell = rho_ref.shape
    cells = cxl * cyl
    nyp = cyl + 2
    nodes = svel_ref.shape[1]
    nhi = nodes // LANES
    ties = 4 * cells
    x, y = lax.axis_index("gx"), lax.axis_index("gy")

    def peer(a, b):
        return (lax.rem(x + a + nx, nx), lax.rem(y + b + ny, ny))

    def slot_of(a, b):
        return (a + 1) * ny + lax.rem(y + b + ny, ny)

    peers = [(a, b) for a in (-1, 0, 1) for b in range(ny) if (a, b) != (0, 0)]
    barrier = pltpu.get_barrier_semaphore()
    for a, b in peers:
        pl.semaphore_signal(barrier, inc=1, device_id=peer(a, b), device_id_type=MESH)

    lane_cell = iota((1, cell), 1)
    for i in range(cxl):
        rows = pl.ds(i * cyl, cyl)
        for c in range(3):
            posS[c, rows, :] = pos_ref[c, i]
            velS[c, rows, :] = vel_ref[c, i]
        rhoS[rows, :] = rho_ref[i]
        for j in range(cyl):
            liveS[pl.ds(i * cyl + j, 1), :] = jnp.where(lane_cell < fill_ref[i, j], 1.0, 0.0).astype(F32)

    def fill_pad(pad):
        def row(i, carry):
            for j in range(cyl):
                one = pl.ds(i * cyl + j, 1)
                for c in range(3):
                    pad[i + 1, j + 1, c : c + 1, :] = posS[c, one, :]
                    pad[i + 1, j + 1, 4 + c : 5 + c, :] = velS[c, one, :]
                pad[i + 1, j + 1, 3:4, :] = liveS[one, :]
                pad[i + 1, j + 1, 7:8, :] = rhoS[one, :]
            return carry

        lax.fori_loop(0, cxl, row, 0)

    def to_rows(source, target, index):
        def step(h, carry):
            at = pl.ds(pl.multiple_of(h * LANES, LANES), LANES)
            for c in range(3):
                if index is None:
                    target[pl.ds(c * nhi + h, 1), :] = source[c : c + 1, at]
                else:
                    target[index, pl.ds(c * nhi + h, 1), :] = source[c : c + 1, at]
            return carry

        lax.fori_loop(0, nhi, step, 0)

    def halo_copies(pad, at):
        def cut(d, size):
            if d == 0:
                return pl.ds(1, size), pl.ds(1, size)
            return (pl.ds(size, 1), pl.ds(0, 1)) if d > 0 else (pl.ds(1, 1), pl.ds(size + 1, 1))

        out = []
        for k, (a, b) in enumerate([d for d in DIRS if d != (0, 0)]):
            (sx, tx), (sy, ty) = cut(a, cxl), cut(b, cyl)
            out.append(
                pltpu.make_async_remote_copy(
                    src_ref=pad.at[sx, sy], dst_ref=pad.at[tx, ty],
                    send_sem=halo_send.at[at, k], recv_sem=halo_recv.at[at, k],
                    device_id=peer(a, b), device_id_type=MESH,
                )
            )
        return out

    def win_copies(win, at):
        return [
            pltpu.make_async_remote_copy(
                src_ref=win.at[1], dst_ref=win.at[1 - a],
                send_sem=win_send.at[at, k], recv_sem=win_recv.at[at, k],
                device_id=peer(a, 0), device_id_type=MESH,
            )
            for k, a in enumerate((-1, 1))
        ]

    def msg_copy(msg, at, k, a, b, slot):
        return pltpu.make_async_remote_copy(
            src_ref=msg.at[ny + y], dst_ref=msg.at[slot],
            send_sem=msg_send.at[at, k], recv_sem=msg_recv.at[at, slot],
            device_id=peer(a, b), device_id_type=MESH,
        )

    fill_pad(pad1)
    to_rows(svel_ref, win1, 1)
    pl.semaphore_wait(barrier, len(peers))
    wins = win_copies(win1, 0)
    for copy in wins:
        copy.start()
    halos = halo_copies(pad1, 0)
    for copy in halos:
        copy.start()

    slots = pairs_ref.shape[1]
    own = iota((cells, slots), 0)
    here = (own // cyl + 1) * nyp + own % cyl + 1
    listed = iota((cells, slots), 1) < counts_ref[0, 1]
    first, second = pairs_ref[0:1, :], pairs_ref[1:2, :]
    for k, (a, b) in enumerate(DIRS):
        if (a, b) == (0, 0):
            alive[k] = jnp.ones((cells, cell), F32)
            continue
        there = here + a * nyp + b
        found = ((first == here) & (second == there)) | ((first == there) & (second == here))
        count = jnp.sum(jnp.where(found & listed, 1.0, 0.0).astype(F32), axis=1, keepdims=True)
        alive[k] = jnp.broadcast_to(count, (cells, cell))

    block = 512

    def springs(disp):
        to_rows(disp, dtab, None)
        dtable[...] = table_of(dtab[...])

        def step(j, carry):
            at = pl.ds(pl.multiple_of(j * block, block), block)
            sums = [jnp.zeros((nhi, block), F32) for c in range(3)]
            for l in range(links_ref.shape[0]):
                index = links_ref[l : l + 1, at]
                low, high = index & (LANES - 1), index >> 7
                hot = jnp.where(iota((LANES, block), 0) == low, 1.0, 0.0).astype(BF16)
                got = dot(dtable[...], jnp.concatenate([hot, hot, hot], axis=0))
                at_high = iota((nhi, block), 0) == high
                for c in range(3):
                    sums[c] = sums[c] + jnp.where(at_high, got[c * nhi : (c + 1) * nhi], 0.0)
            for c in range(3):
                beside[c : c + 1, at] = jnp.sum(sums[c], axis=0, keepdims=True)
            return carry

        lax.fori_loop(0, nodes // block, step, 0)

    id_row, weight_row = ties_ref[0:1, :], ties_ref[1:2, :]
    diag = iota((ties, LANES), 0) == iota((ties, LANES), 1)
    id_col = jnp.sum(jnp.where(diag, id_row, 0.0), axis=1, keepdims=True)
    weight_col = jnp.sum(jnp.where(diag, weight_row, 0.0), axis=1, keepdims=True)

    def wall(win, msg, at):
        place = id_col.astype(jnp.int32) - (x - 1) * nodes
        low, high = place & (LANES - 1), place >> 7
        hot = jnp.where(iota((ties, LANES), 1) == low, 1.0, 0.0).astype(BF16)
        hot = jnp.concatenate([hot, hot, hot], axis=1)
        value = [jnp.zeros((ties, 1), F32) for c in range(3)]
        lane = iota((ties, 3 * nhi), 1)
        for strip in range(3):
            got = dot_t(hot, table_of(win[strip]))
            inside = high - strip * nhi
            fits = (inside >= 0) & (inside < nhi)
            for c in range(3):
                pick = fits & (lane == inside + c * nhi)
                value[c] = value[c] + jnp.sum(jnp.where(pick, got, 0.0), axis=1, keepdims=True)
        contact = jnp.maximum(1.0 - 2.0 * posS[2], 0.0)
        contact = contact * contact * liveS[...]
        mine = ny + y
        msg[mine] = jnp.zeros((8, LANES), F32)
        spread = iota((cells, LANES), 0) == (iota((cells, LANES), 1) & (cells - 1))
        for c in range(3):
            tied = value[c] * weight_col
            coupled = sum(tied[k * cells : (k + 1) * cells] for k in range(4))
            push = 0.2 * contact * (coupled - velS[c])
            if c == 2:
                push = push + 0.1 * contact
            pushS[c] = push
            load = -jnp.sum(push, axis=1, keepdims=True)
            row = jnp.sum(jnp.where(spread, load, 0.0), axis=0, keepdims=True)
            msg[mine, c : c + 1, :] = row * weight_row
        msg[mine, 3:4, :] = id_row
        for k, (a, b) in enumerate(peers):
            msg_copy(msg, at, k, a, b, (1 - a) * ny + y).start()

    def shell_step(msg, at, speed, disp):
        for k, (a, b) in enumerate(peers):
            msg_copy(msg, at, k, a, b, slot_of(a, b)).wait_recv()

        def add(s, total):
            note = msg[s]
            place = note[3:4].astype(jnp.int32) - x * nodes
            low, high = place & (LANES - 1), place >> 7
            at_high = iota((nhi, LANES), 0) == high
            share = jnp.concatenate([jnp.where(at_high, note[c : c + 1], 0.0) for c in range(3)], axis=0)
            hot = jnp.where(iota((LANES, LANES), 0) == low, 1.0, 0.0).astype(BF16)
            return total + dot_t(table_of(share), jnp.concatenate([hot, hot, hot], axis=1))

        dtab[...] = lax.fori_loop(0, 3 * ny, add, jnp.zeros((3 * nhi, LANES), F32))

        def row(h, carry):
            for c in range(3):
                node[c : c + 1, pl.ds(pl.multiple_of(h * LANES, LANES), LANES)] = dtab[pl.ds(c * nhi + h, 1), :]
            return carry

        lax.fori_loop(0, nhi, row, 0)
        old = disp[...]
        spring = 4.0 * old - beside[...]
        new = speed[...] + 0.5 * (0.2 * node[...] - 0.5 * spring)
        speed_out[...] = new
        offset_out[...] = old + 0.5 * new

    row8 = iota((8, cell), 0)

    def geometry(pad, i, j):
        field = pad[i, j]
        shift_x = (i - 3).astype(F32) if not isinstance(i, int) else float(i - 3)
        shift_y = (j - 3).astype(F32) if not isinstance(j, int) else float(j - 3)
        shift = jnp.where(row8 == 0, shift_x, jnp.where(row8 == 1, shift_y, -0.5))
        xyz = jnp.where(row8 < 3, field + shift, 0.0)
        return field, xyz

    def along(field, xyz):
        return xyz[0:1] * field[4:5] + xyz[1:2] * field[5:6] + xyz[2:3] * field[6:7]

    def geo_tables(pad):
        def step(p, carry):
            field, xyz = geometry(pad, p // nyp, p % nyp)
            square = jnp.sum(xyz * xyz, axis=0, keepdims=True)
            to = jnp.where(row8 < 3, xyz, jnp.where(row8 == 3, 1.0 - square, jnp.where(row8 == 4, -1.0, 0.0)))
            by = jnp.where(row8 < 3, 2.0 * xyz, jnp.where(row8 == 3, 1.0, jnp.where(row8 == 4, square, 0.0)))
            th, tm, tl = split3(to)
            bh, bm, bl = split3(by)
            right[p] = jnp.concatenate([th, tm, th, tm, tl, th], axis=0).astype(BF16)
            turned = jnp.concatenate([bh, bh, bm, bm, bh, bl] + [jnp.zeros((8, cell), F32)] * 10, axis=0)
            left[p] = jnp.transpose(turned)[:, :48].astype(BF16)
            return carry

        lax.fori_loop(0, (cxl + 2) * nyp, step, 0)

    def load_tables(pad):
        def step(p, carry):
            field, xyz = geometry(pad, p // nyp, p % nyp)
            live, press = field[3:4], 2.0 * (field[7:8] - 1.0)
            flat = jnp.where(row8 < 3, xyz, jnp.where(row8 == 3, 1.0, jnp.where(row8 == 7, along(field, xyz), field)))
            flat = flat * live
            pressed = jnp.where(row8 < 4, flat, 0.0) * press
            fh, fm, fl = split3(flat)
            ph, pm, pm2 = split3(pressed)
            loads[p] = jnp.concatenate([fh, ph, fm, pm, fl, pm2], axis=0).astype(BF16)
            return carry

        lax.fori_loop(0, (cxl + 2) * nyp, step, 0)

    chunk = 64

    def forces(pad, fresh):
        def step(own_cell, carry):
            i, j = own_cell // cyl + 1, own_cell % cyl + 1
            here = i * nyp + j
            total = jnp.zeros((48, cell), F32)
            for k, (a, b) in enumerate(DIRS):
                there = here + a * nyp + b
                tile = own_cell * 9 + k
                if fresh:
                    for s in range(cell // chunk):
                        part = pl.ds(s * chunk, chunk)
                        close = jnp.maximum(dot(left[there, part, :], right[here]), 0.0)
                        weight = close * close
                        high = weight.astype(BF16)
                        whigh[tile, part, :] = high
                        wlow[tile, part, :] = (weight - high.astype(F32)).astype(BF16)
                summed = dot(loads[there], whigh[tile]) + dot(loads[there], wlow[tile])
                total = total + summed * alive[k, pl.ds(own_cell, 1), :]
            total = total[0:16] + total[16:32] + total[32:48]
            field, xyz = geometry(pad, i, j)
            live, press = field[3:4], 2.0 * (field[7:8] - 1.0)
            count, pressure = total[3:4], total[11:12]
            rate = along(field, xyz) * count + total[7:8]
            for c in range(3):
                at, speed = xyz[c : c + 1], field[4 + c : 5 + c]
                moved, sped = total[c : c + 1], total[4 + c : 5 + c]
                push = press * (at * count - moved) + at * pressure - total[8 + c : 9 + c]
                push = push - 0.5 * (speed * count - sped)
                forS[c, pl.ds(own_cell, 1), :] = push * live
                rate = rate - speed * moved - at * sped
            forS[3, pl.ds(own_cell, 1), :] = rate * live
            return carry

        lax.fori_loop(0, cells, step, 0)

    def advance():
        for c in range(3):
            velS[c] = velS[c] + 0.5 * (0.02 * forS[c] + pushS[c])
        rhoS[...] = rhoS[...] + 0.5 * 0.02 * forS[3]

    springs(disp_ref)
    for copy in wins:
        copy.wait_recv()
    wall(win1, msg1, 0)
    for copy in halos:
        copy.wait_recv()
    geo_tables(pad1)
    load_tables(pad1)
    forces(pad1, True)
    advance()
    fill_pad(pad2)
    halos2 = halo_copies(pad2, 1)
    for copy in halos2:
        copy.start()
    shell_step(msg1, 0, svel_ref, disp_ref)
    to_rows(speed_out, win2, 1)
    wins2 = win_copies(win2, 1)
    for copy in wins2:
        copy.start()
    springs(offset_out)
    for copy in wins2:
        copy.wait_recv()
    wall(win2, msg2, 1)
    for copy in halos2:
        copy.wait_recv()
    load_tables(pad2)
    forces(pad2, False)
    advance()
    for i in range(cxl):
        rows = pl.ds(i * cyl, cyl)
        for c in range(3):
            vel_out[c, i] = velS[c, rows, :]
        rho_out[i] = rhoS[rows, :]
    shell_step(msg2, 1, speed_out, offset_out)
    for copy in wins + halos + wins2 + halos2:
        copy.wait_send()
    for at, msg in enumerate((msg1, msg2)):
        for k, (a, b) in enumerate(peers):
            msg_copy(msg, at, k, a, b, slot_of(a, b)).wait_send()


def body(nx, ny, positions, velocity, density, cell_fill, pair_cells, pair_counts,
         shell_nodes, shell_weights, shell_links, shell_disp, shell_vel):
    cxl, cyl, cell = density.shape
    cells, pads = cxl * cyl, (cxl + 2) * (cyl + 2)
    nodes = shell_vel.shape[1]
    nhi = nodes // LANES
    entries = shell_nodes.size
    ties = jnp.stack([shell_nodes.reshape(-1).astype(F32), shell_weights.reshape(-1)])
    ties = jnp.pad(ties, ((0, 6), (0, LANES - entries)))
    npeers = 3 * ny
    vmem = pl.BlockSpec(memory_space=pltpu.VMEM)
    smem = pl.BlockSpec(memory_space=pltpu.SMEM)
    return pl.pallas_call(
        functools.partial(kernel, nx, ny),
        out_shape=[
            jax.ShapeDtypeStruct(velocity.shape, F32),
            jax.ShapeDtypeStruct(density.shape, F32),
            jax.ShapeDtypeStruct(shell_vel.shape, F32),
            jax.ShapeDtypeStruct(shell_disp.shape, F32),
        ],
        in_specs=[vmem, vmem, vmem, smem, vmem, smem, vmem, vmem, vmem, vmem],
        out_specs=[vmem] * 4,
        scratch_shapes=[
            pltpu.VMEM((3, cells, cell), F32),
            pltpu.VMEM((3, cells, cell), F32),
            pltpu.VMEM((cells, cell), F32),
            pltpu.VMEM((cells, cell), F32),
            pltpu.VMEM((3, cells, cell), F32),
            pltpu.VMEM((4, cells, cell), F32),
            pltpu.VMEM((cxl + 2, cyl + 2, 8, cell), F32),
            pltpu.VMEM((cxl + 2, cyl + 2, 8, cell), F32),
            pltpu.VMEM((3, 3 * nhi, LANES), F32),
            pltpu.VMEM((3, 3 * nhi, LANES), F32),
            pltpu.VMEM((npeers, 8, LANES), F32),
            pltpu.VMEM((npeers, 8, LANES), F32),
            pltpu.VMEM((9, cells, cell), F32),
            pltpu.VMEM((3 * nhi, LANES), F32),
            pltpu.VMEM((3 * nhi, 3 * LANES), BF16),
            pltpu.VMEM((3, nodes), F32),
            pltpu.VMEM((3, nodes), F32),
            pltpu.VMEM((pads, cell, 48), BF16),
            pltpu.VMEM((pads, 48, cell), BF16),
            pltpu.VMEM((pads, 48, cell), BF16),
            pltpu.VMEM((cells * 9, cell, cell), BF16),
            pltpu.VMEM((cells * 9, cell, cell), BF16),
            pltpu.SemaphoreType.DMA((2, 8)),
            pltpu.SemaphoreType.DMA((2, 8)),
            pltpu.SemaphoreType.DMA((2, 2)),
            pltpu.SemaphoreType.DMA((2, 2)),
            pltpu.SemaphoreType.DMA((2, npeers)),
            pltpu.SemaphoreType.DMA((2, npeers)),
        ],
        compiler_params=pltpu.CompilerParams(
            collective_id=0, has_side_effects=True, vmem_limit_bytes=56 * 1024 * 1024
        ),
        name="hydro",
    )(positions, velocity, density, cell_fill, pair_cells[0, 0], pair_counts[0], ties,
      shell_links, shell_disp, shell_vel)


def solution(mesh):
    nx, ny = mesh.shape["gx"], mesh.shape["gy"]
    return jax.shard_map(
        functools.partial(body, nx, ny),
        mesh=mesh,
        in_specs=(
            P(None, "gx", "gy", None),
            P(None, "gx", "gy", None),
            P("gx", "gy", None),
            P("gx", "gy"),
            P("gx", "gy", None, None),
            P("gx", "gy", None),
            P(None, "gx", "gy"),
            P(None, "gx", "gy"),
            P(None, "gx"),
            P(None, "gx"),
            P(None, "gx"),
        ),
        out_specs=(P(None, "gx", "gy", None), P("gx", "gy", None), P(None, "gx"), P(None, "gx")),
        check_vma=False,
    )
```

time: 621 us -> 62.7 us (0.10)
  local copies, waits for them, and re-layouts: 272 us -> 4.44 us
  other arithmetic: 167 us -> 0.61 us
  starting transfers between devices: 113 us -> 0 us
  Pallas kernels: 0 us -> 56.7 us
  blocking collectives: 33.3 us -> 0 us
  waiting for transfers between devices: 22.8 us -> 0 us
    gather x196 -> x0, local copies, waits for them, and re-layouts: 230 us -> none  [the longest x2 109 us: shell_update(): beside_all = jnp.sum(disp[:, links], 1)]
    ppermute x28 -> x0, starting transfers between devices: 113 us -> none  [the longest x14 94.9 us: with_halo(): before = lax.ppermute(last, axis, up)]
    reduce_sum x42 -> x0, other arithmetic: 96.6 us -> none  [the longest x28 68.5 us: pair_terms(): jnp.sum(fields[0], 0)]
    pallas_call x0 -> x1, Pallas kernels: none -> 56.7 us  [body(): pl.pallas_call(functools.partial(kernel, nx, ny), out_shape=[jax.ShapeDty...]
    scatter-add x73 -> x0, other arithmetic: 49.6 us -> none  [the longest x28 18.3 us: pair_turn(): sums = sums.at[first].add(row_sums * valid[:, None, None])]
    psum x2 -> x0, blocking collectives: 33.3 us -> none  [body(): node_force = lax.psum(strip_part, 'gy')]
    ppermute x28 -> x0, waiting for transfers between devices: 22.8 us -> none  [the longest x14 20.2 us: with_halo(): after = lax.ppermute(first, axis, down)]
    slice x77 -> x0, local copies, waits for them, and re-layouts: 18.9 us -> none  [the longest x4 13.4 us: with_halo(): last = lax.slice_in_dim(shard, length - width, length, axis=dim)]
  transfers between devices with their start and end apart: 28 -> 0, of which waited for: 7 -> 0; matrix products, arithmetic and copies ran while one was open for 50% -> 0% of each run, Pallas kernels for 0% -> 0%
where the time goes in v1:
time: 62.7 us; the launch traced here: 62.4 us
  Pallas kernels  56.7 us (90%)
  local copies, waits for them, and re-layouts  4.44 us (7%)
  between operations  0.69 us (1%)
    pallas_call x1, Pallas kernels, body(): pl.pallas_call(functools.partial(kernel, nx, ny), out_shape=[jax.ShapeDty...  56.7 us
    unnamed x12, local copies, waits for them, and re-layouts  3.56 us

profile of v1, /device:TPU:0, one launch (start us, length us, event | category | flops | bytes accessed | tf_op | source)
XLA Modules:
  0.0 62.4 jit_solution(2906111790292748828)
XLA Ops:
  0.6 0.0 copy-start.3
  0.6 0.8 %stack_reshape.3 = f32[1,64]{1,0:T(1,128)S(1)} reshape(f32[4,4,4]{2,1,0:T(4,128)} %param.18) | data formatting | bytes 512 | tf_op jit(solution)/shard_map/stack;reshape | solution.py:382
  1.4 0.0 copy-done.3
  1.5 0.1 convert_element_type.16
  1.5 0.6 select_maximum_fusion.ties_ref
  2.2 56.7 %hydro.1 = (f32[3,4,4,256]{3,2,1,0:T(4,128)}, f32[4,4,256]{2,1,0:T(4,128)}, f32[3,4096]{1,0:T(4,128)}, f32[3,4096]{1,0:T(4,128)}) custom-call(f32[3,4,4,256]{3,2,1,0:T(4,128)} %pos_ref.1, f32[3,4,4,256]{3,2,1,0:T(4,128)} %vel_ref.1, f32[4,4,256]{2,1,0:T(4,128)} %rho_ref.1, s32[4,4]{1,0:T(4,128)} %fill_ref.1, s32[2,86]{1,0:T(2,128)} %bitcast.2, ...), custom_call_target="tpu_custom_call" | custom-call | tf_op jit(solution)/shard_map/hydro/pallas_call | solution.py:387
  58.8 0.0 copy-start.2
  58.9 0.0 copy-start.1
  58.9 1.5 %copy.19 = f32[3,4,4,256]{3,2,1,0:T(4,128)} copy(f32[3,4,4,256]{3,2,1,0:T(4,128)} %get-tuple-element.8) | data formatting | bytes 98304
  60.3 0.0 copy-done.2
  60.3 0.6 copy.20
  60.9 0.0 copy-done.1
  60.9 0.0 copy-start
  60.9 0.6 %copy.21 = f32[3,4096]{1,0:T(4,128)} copy(f32[3,4096]{1,0:T(4,128)S(1)} %copy-done.1) | data formatting | bytes 98304
  61.6 0.2 copy-done
  61.8 0.6 %copy.22 = f32[3,4096]{1,0:T(4,128)} copy(f32[3,4096]{1,0:T(4,128)S(1)} %copy-done) | data formatting | bytes 98304
  (1 shorter events, 0.0 us)
Async XLA Ops:
  0.6 0.8 %copy-start.3 = (s32[4,4,4]{2,1,0:T(4,128)S(1)}, s32[4,4,4]{2,1,0:T(4,128)}, u32[]{:S(2)}) copy-start(s32[4,4,4]{2,1,0:T(4,128)} %param.17) | copy-start | bytes 772
  58.8 1.5 %copy-start.2 = (f32[4,4,256]{2,1,0:T(4,128)S(1)}, f32[4,4,256]{2,1,0:T(4,128)}, u32[]{:S(2)}) copy-start(f32[4,4,256]{2,1,0:T(4,128)} %get-tuple-element.9) | copy-start | bytes 49156
  58.9 2.1 %copy-start.1 = (f32[3,4096]{1,0:T(4,128)S(1)}, f32[3,4096]{1,0:T(4,128)}, u32[]{:S(2)}) copy-start(f32[3,4096]{1,0:T(4,128)} %get-tuple-element.10) | copy-start | bytes 147460
  60.9 0.9 %copy-start = (f32[3,4096]{1,0:T(4,128)S(1)}, f32[3,4096]{1,0:T(4,128)}, u32[]{:S(2)}) copy-start(f32[3,4096]{1,0:T(4,128)} %get-tuple-element.11) | copy-start | bytes 147460

commit v2 on v1

--- a/solution.py
+++ b/solution.py
@@ -43,7 +43,7 @@
     pos_ref, vel_ref, rho_ref, fill_ref, pairs_ref, counts_ref, ties_ref, links_ref, disp_ref, svel_ref,
     vel_out, rho_out, speed_out, offset_out,
     posS, velS, rhoS, liveS, pushS, forS, pad1, pad2, win1, win2, msg1, msg2,
-    alive, dtab, dtable, beside, node, left, right, loads, whigh, wlow,
+    alive, dtab, dtable, beside, node, left, right, loads, whigh, wlow, totals,
     halo_send, halo_recv, win_send, win_recv, msg_send, msg_recv,
 ):
     cxl, cyl, cell = rho_ref.shape
@@ -86,7 +86,7 @@
                 pad[i + 1, j + 1, 7:8, :] = rhoS[one, :]
             return carry
 
-        lax.fori_loop(0, cxl, row, 0)
+        lax.fori_loop(0, cxl, row, 0, unroll=True)
 
     def to_rows(source, target, index):
         def step(h, carry):
@@ -98,7 +98,7 @@
                     target[index, pl.ds(c * nhi + h, 1), :] = source[c : c + 1, at]
             return carry
 
-        lax.fori_loop(0, nhi, step, 0)
+        lax.fori_loop(0, nhi, step, 0, unroll=8)
 
     def halo_copies(pad, at):
         def cut(d, size):
@@ -233,14 +233,14 @@
             hot = jnp.where(iota((LANES, LANES), 0) == low, 1.0, 0.0).astype(BF16)
             return total + dot_t(table_of(share), jnp.concatenate([hot, hot, hot], axis=1))
 
-        dtab[...] = lax.fori_loop(0, 3 * ny, add, jnp.zeros((3 * nhi, LANES), F32))
+        dtab[...] = lax.fori_loop(0, 3 * ny, add, jnp.zeros((3 * nhi, LANES), F32), unroll=6)
 
         def row(h, carry):
             for c in range(3):
                 node[c : c + 1, pl.ds(pl.multiple_of(h * LANES, LANES), LANES)] = dtab[pl.ds(c * nhi + h, 1), :]
             return carry
 
-        lax.fori_loop(0, nhi, row, 0)
+        lax.fori_loop(0, nhi, row, 0, unroll=8)
         old = disp[...]
         spring = 4.0 * old - beside[...]
         new = speed[...] + 0.5 * (0.2 * node[...] - 0.5 * spring)
@@ -260,9 +260,31 @@
     def along(field, xyz):
         return xyz[0:1] * field[4:5] + xyz[1:2] * field[5:6] + xyz[2:3] * field[6:7]
 
-    def geo_tables(pad):
-        def step(p, carry):
-            field, xyz = geometry(pad, p // nyp, p % nyp)
+    def each_own(step):
+        def one(c, carry):
+            step(c // cyl + 1, c % cyl + 1)
+            return carry
+
+        lax.fori_loop(0, cells, one, 0, unroll=4)
+
+    def each_halo(step):
+        def across(j, carry):
+            step(0, j)
+            step(cxl + 1, j)
+            return carry
+
+        def beside_it(i, carry):
+            step(i, 0)
+            step(i, cyl + 1)
+            return carry
+
+        lax.fori_loop(0, nyp, across, 0, unroll=2)
+        lax.fori_loop(1, cxl + 1, beside_it, 0, unroll=2)
+
+    def geo_tables(pad, each):
+        def step(i, j):
+            p = i * nyp + j
+            field, xyz = geometry(pad, i, j)
             square = jnp.sum(xyz * xyz, axis=0, keepdims=True)
             to = jnp.where(row8 < 3, xyz, jnp.where(row8 == 3, 1.0 - square, jnp.where(row8 == 4, -1.0, 0.0)))
             by = jnp.where(row8 < 3, 2.0 * xyz, jnp.where(row8 == 3, 1.0, jnp.where(row8 == 4, square, 0.0)))
@@ -271,13 +293,13 @@
             right[p] = jnp.concatenate([th, tm, th, tm, tl, th], axis=0).astype(BF16)
             turned = jnp.concatenate([bh, bh, bm, bm, bh, bl] + [jnp.zeros((8, cell), F32)] * 10, axis=0)
             left[p] = jnp.transpose(turned)[:, :48].astype(BF16)
-            return carry
-
-        lax.fori_loop(0, (cxl + 2) * nyp, step, 0)
-
-    def load_tables(pad):
-        def step(p, carry):
-            field, xyz = geometry(pad, p // nyp, p % nyp)
+
+        each(step)
+
+    def load_tables(pad, each):
+        def step(i, j):
+            p = i * nyp + j
+            field, xyz = geometry(pad, i, j)
             live, press = field[3:4], 2.0 * (field[7:8] - 1.0)
             flat = jnp.where(row8 < 3, xyz, jnp.where(row8 == 3, 1.0, jnp.where(row8 == 7, along(field, xyz), field)))
             flat = flat * live
@@ -285,46 +307,60 @@
             fh, fm, fl = split3(flat)
             ph, pm, pm2 = split3(pressed)
             loads[p] = jnp.concatenate([fh, ph, fm, pm, fl, pm2], axis=0).astype(BF16)
-            return carry
-
-        lax.fori_loop(0, (cxl + 2) * nyp, step, 0)
+
+        each(step)
 
     chunk = 64
 
-    def forces(pad, fresh):
+    def weights():
         def step(own_cell, carry):
-            i, j = own_cell // cyl + 1, own_cell % cyl + 1
-            here = i * nyp + j
+            here = (own_cell // cyl + 1) * nyp + own_cell % cyl + 1
+            for k, (a, b) in enumerate(DIRS):
+                there = here + a * nyp + b
+                for s in range(cell // chunk):
+                    part = pl.ds(s * chunk, chunk)
+                    close = jnp.maximum(dot(left[there, part, :], right[here]), 0.0)
+                    weight = close * close
+                    high = weight.astype(BF16)
+                    whigh[own_cell * 9 + k, part, :] = high
+                    if (a, b) == (0, 0):
+                        wlow[own_cell, part, :] = (weight - high.astype(F32)).astype(BF16)
+            return carry
+
+        lax.fori_loop(0, cells, step, 0)
+
+    def forces():
+        def step(own_cell, carry):
+            here = (own_cell // cyl + 1) * nyp + own_cell % cyl + 1
             total = jnp.zeros((48, cell), F32)
             for k, (a, b) in enumerate(DIRS):
                 there = here + a * nyp + b
-                tile = own_cell * 9 + k
-                if fresh:
-                    for s in range(cell // chunk):
-                        part = pl.ds(s * chunk, chunk)
-                        close = jnp.maximum(dot(left[there, part, :], right[here]), 0.0)
-                        weight = close * close
-                        high = weight.astype(BF16)
-                        whigh[tile, part, :] = high
-                        wlow[tile, part, :] = (weight - high.astype(F32)).astype(BF16)
-                summed = dot(loads[there], whigh[tile]) + dot(loads[there], wlow[tile])
-                total = total + summed * alive[k, pl.ds(own_cell, 1), :]
+                summed = dot(loads[there], whigh[own_cell * 9 + k])
+                if (a, b) == (0, 0):
+                    total = total + (summed + dot(loads[there], wlow[own_cell]))
+                else:
+                    total = total + summed * alive[k, pl.ds(own_cell, 1), :]
             total = total[0:16] + total[16:32] + total[32:48]
-            field, xyz = geometry(pad, i, j)
-            live, press = field[3:4], 2.0 * (field[7:8] - 1.0)
-            count, pressure = total[3:4], total[11:12]
-            rate = along(field, xyz) * count + total[7:8]
-            for c in range(3):
-                at, speed = xyz[c : c + 1], field[4 + c : 5 + c]
-                moved, sped = total[c : c + 1], total[4 + c : 5 + c]
-                push = press * (at * count - moved) + at * pressure - total[8 + c : 9 + c]
-                push = push - 0.5 * (speed * count - sped)
-                forS[c, pl.ds(own_cell, 1), :] = push * live
-                rate = rate - speed * moved - at * sped
-            forS[3, pl.ds(own_cell, 1), :] = rate * live
-            return carry
-
-        lax.fori_loop(0, cells, step, 0)
+            for c in range(12):
+                totals[c, pl.ds(own_cell, 1), :] = total[c : c + 1]
+            return carry
+
+        lax.fori_loop(0, cells, step, 0, unroll=2)
+        live, press = liveS[...], 2.0 * (rhoS[...] - 1.0)
+        count, pressure = totals[3], totals[11]
+        own_cell = iota((cells, cell), 0)
+        spot = [
+            posS[0] + (own_cell // cyl - 2).astype(F32),
+            posS[1] + (own_cell % cyl - 2).astype(F32),
+            posS[2] - 0.5,
+        ]
+        rate = (spot[0] * velS[0] + spot[1] * velS[1] + spot[2] * velS[2]) * count + totals[7]
+        for c in range(3):
+            push = press * (spot[c] * count - totals[c]) + spot[c] * pressure - totals[8 + c]
+            push = push - 0.5 * (velS[c] * count - totals[4 + c])
+            forS[c] = push * live
+            rate = rate - velS[c] * totals[c] - spot[c] * totals[4 + c]
+        forS[3] = rate * live
 
     def advance():
         for c in range(3):
@@ -332,14 +368,17 @@
         rhoS[...] = rhoS[...] + 0.5 * 0.02 * forS[3]
 
     springs(disp_ref)
+    geo_tables(pad1, each_own)
+    load_tables(pad1, each_own)
     for copy in wins:
         copy.wait_recv()
     wall(win1, msg1, 0)
     for copy in halos:
         copy.wait_recv()
-    geo_tables(pad1)
-    load_tables(pad1)
-    forces(pad1, True)
+    geo_tables(pad1, each_halo)
+    load_tables(pad1, each_halo)
+    weights()
+    forces()
     advance()
     fill_pad(pad2)
     halos2 = halo_copies(pad2, 1)
@@ -351,13 +390,14 @@
     for copy in wins2:
         copy.start()
     springs(offset_out)
+    load_tables(pad2, each_own)
     for copy in wins2:
         copy.wait_recv()
     wall(win2, msg2, 1)
     for copy in halos2:
         copy.wait_recv()
-    load_tables(pad2)
-    forces(pad2, False)
+    load_tables(pad2, each_halo)
+    forces()
     advance()
     for i in range(cxl):
         rows = pl.ds(i * cyl, cyl)
@@ -416,7 +456,8 @@
             pltpu.VMEM((pads, 48, cell), BF16),
             pltpu.VMEM((pads, 48, cell), BF16),
             pltpu.VMEM((cells * 9, cell, cell), BF16),
-            pltpu.VMEM((cells * 9, cell, cell), BF16),
+            pltpu.VMEM((cells, cell, cell), BF16),
+            pltpu.VMEM((12, cells, cell), F32),
             pltpu.SemaphoreType.DMA((2, 8)),
             pltpu.SemaphoreType.DMA((2, 8)),
             pltpu.SemaphoreType.DMA((2, 2)),

time: 62.7 us -> 44.6 us (0.71)
  Pallas kernels: 56.7 us -> 38.6 us
    pallas_call x1, Pallas kernels: 56.7 us -> 38.6 us  [body(): pl.pallas_call(functools.partial(kernel, nx, ny), out_shape=[jax.ShapeDty...]
where the time goes in v2:
time: 44.6 us; the launch traced here: 44.3 us
  Pallas kernels  38.6 us (87%)
  local copies, waits for them, and re-layouts  4.44 us (10%)
  between operations  0.69 us (2%)
  other arithmetic  0.61 us (1%)
    pallas_call x1, Pallas kernels, body(): pl.pallas_call(functools.partial(kernel, nx, ny), out_shape=[jax.ShapeDty...  38.6 us
    unnamed x12, local copies, waits for them, and re-layouts  3.56 us

profile of v2, /device:TPU:0, one launch (start us, length us, event | category | flops | bytes accessed | tf_op | source)
XLA Modules:
  0.0 44.3 jit_solution(356963175030077745)
XLA Ops:
  0.6 0.0 copy-start.3
  0.6 0.8 %stack_reshape.3 = f32[1,64]{1,0:T(1,128)S(1)} reshape(f32[4,4,4]{2,1,0:T(4,128)} %param.18) | data formatting | bytes 512 | tf_op jit(solution)/shard_map/stack;reshape | solution.py:422
  1.4 0.0 copy-done.3
  1.5 0.1 convert_element_type.16
  1.5 0.6 %select_maximum_fusion.ties_ref = f32[8,128]{1,0:T(8,128)} fusion(f32[1,64]{1,0:T(1,128)S(1)} %stack_reshape.3, f32[1,64]{1,0:T(1,128)S(1)} %convert_element_type.16), kind=kLoop, calls=%fused_computation | loop fusion | flops 8192 | bytes 4608 | tf_op jit(solution)/shard_map/stack | solution.py:422
  2.2 38.6 %hydro.1 = (f32[3,4,4,256]{3,2,1,0:T(4,128)}, f32[4,4,256]{2,1,0:T(4,128)}, f32[3,4096]{1,0:T(4,128)}, f32[3,4096]{1,0:T(4,128)}) custom-call(f32[3,4,4,256]{3,2,1,0:T(4,128)} %pos_ref.1, f32[3,4,4,256]{3,2,1,0:T(4,128)} %vel_ref.1, f32[4,4,256]{2,1,0:T(4,128)} %rho_ref.1, s32[4,4]{1,0:T(4,128)} %fill_ref.1, s32[2,86]{1,0:T(2,128)} %bitcast.2, ...), custom_call_target="tpu_custom_call" | custom-call | tf_op jit(solution)/shard_map/hydro/pallas_call | solution.py:427
  40.7 0.0 copy-start.2
  40.7 0.0 copy-start.1
  40.8 1.5 %copy.19 = f32[3,4,4,256]{3,2,1,0:T(4,128)} copy(f32[3,4,4,256]{3,2,1,0:T(4,128)} %get-tuple-element.8) | data formatting | bytes 98304
  42.2 0.0 copy-done.2
  42.2 0.6 %copy.20 = f32[4,4,256]{2,1,0:T(4,128)} copy(f32[4,4,256]{2,1,0:T(4,128)S(1)} %copy-done.2) | data formatting | bytes 32768
  42.8 0.0 copy-done.1
  42.8 0.0 copy-start
  42.8 0.6 %copy.21 = f32[3,4096]{1,0:T(4,128)} copy(f32[3,4096]{1,0:T(4,128)S(1)} %copy-done.1) | data formatting | bytes 98304
  43.5 0.2 copy-done
  43.7 0.6 %copy.22 = f32[3,4096]{1,0:T(4,128)} copy(f32[3,4096]{1,0:T(4,128)S(1)} %copy-done) | data formatting | bytes 98304
  (1 shorter events, 0.0 us)
Async XLA Ops:
  0.6 0.8 %copy-start.3 = (s32[4,4,4]{2,1,0:T(4,128)S(1)}, s32[4,4,4]{2,1,0:T(4,128)}, u32[]{:S(2)}) copy-start(s32[4,4,4]{2,1,0:T(4,128)} %param.17) | copy-start | bytes 772
  40.7 1.5 %copy-start.2 = (f32[4,4,256]{2,1,0:T(4,128)S(1)}, f32[4,4,256]{2,1,0:T(4,128)}, u32[]{:S(2)}) copy-start(f32[4,4,256]{2,1,0:T(4,128)} %get-tuple-element.9) | copy-start | bytes 49156
  40.7 2.1 %copy-start.1 = (f32[3,4096]{1,0:T(4,128)S(1)}, f32[3,4096]{1,0:T(4,128)}, u32[]{:S(2)}) copy-start(f32[3,4096]{1,0:T(4,128)} %get-tuple-element.10) | copy-start | bytes 147460
  42.8 0.9 %copy-start = (f32[3,4096]{1,0:T(4,128)S(1)}, f32[3,4096]{1,0:T(4,128)}, u32[]{:S(2)}) copy-start(f32[3,4096]{1,0:T(4,128)} %get-tuple-element.11) | copy-start | bytes 147460

commit v3 on v2

--- a/solution.py
+++ b/solution.py
@@ -180,7 +180,7 @@
                 beside[c : c + 1, at] = jnp.sum(sums[c], axis=0, keepdims=True)
             return carry
 
-        lax.fori_loop(0, nodes // block, step, 0)
+        lax.fori_loop(0, nodes // block, step, 0, unroll=2)
 
     id_row, weight_row = ties_ref[0:1, :], ties_ref[1:2, :]
     diag = iota((ties, LANES), 0) == iota((ties, LANES), 1)
@@ -233,7 +233,7 @@
             hot = jnp.where(iota((LANES, LANES), 0) == low, 1.0, 0.0).astype(BF16)
             return total + dot_t(table_of(share), jnp.concatenate([hot, hot, hot], axis=1))
 
-        dtab[...] = lax.fori_loop(0, 3 * ny, add, jnp.zeros((3 * nhi, LANES), F32), unroll=6)
+        dtab[...] = lax.fori_loop(0, 3 * ny, add, jnp.zeros((3 * nhi, LANES), F32), unroll=True)
 
         def row(h, carry):
             for c in range(3):
@@ -327,7 +327,7 @@
                         wlow[own_cell, part, :] = (weight - high.astype(F32)).astype(BF16)
             return carry
 
-        lax.fori_loop(0, cells, step, 0)
+        lax.fori_loop(0, cells, step, 0, unroll=2)
 
     def forces():
         def step(own_cell, carry):
@@ -345,7 +345,7 @@
                 totals[c, pl.ds(own_cell, 1), :] = total[c : c + 1]
             return carry
 
-        lax.fori_loop(0, cells, step, 0, unroll=2)
+        lax.fori_loop(0, cells, step, 0, unroll=4)
         live, press = liveS[...], 2.0 * (rhoS[...] - 1.0)
         count, pressure = totals[3], totals[11]
         own_cell = iota((cells, cell), 0)
@@ -368,13 +368,13 @@
         rhoS[...] = rhoS[...] + 0.5 * 0.02 * forS[3]
 
     springs(disp_ref)
-    geo_tables(pad1, each_own)
-    load_tables(pad1, each_own)
     for copy in wins:
         copy.wait_recv()
     wall(win1, msg1, 0)
     for copy in halos:
         copy.wait_recv()
+    geo_tables(pad1, each_own)
+    load_tables(pad1, each_own)
     geo_tables(pad1, each_halo)
     load_tables(pad1, each_halo)
     weights()
@@ -390,12 +390,12 @@
     for copy in wins2:
         copy.start()
     springs(offset_out)
-    load_tables(pad2, each_own)
     for copy in wins2:
         copy.wait_recv()
     wall(win2, msg2, 1)
     for copy in halos2:
         copy.wait_recv()
+    load_tables(pad2, each_own)
     load_tables(pad2, each_halo)
     forces()
     advance()

time: 44.6 us -> 41.9 us (0.939)
  Pallas kernels: 38.6 us -> 35.8 us
    pallas_call x1, Pallas kernels: 38.6 us -> 35.8 us  [body(): pl.pallas_call(functools.partial(kernel, nx, ny), out_shape=[jax.ShapeDty...]
where the time goes in v3:
time: 41.9 us; the launch traced here: 41.6 us
  Pallas kernels  35.8 us (85%)
  local copies, waits for them, and re-layouts  4.44 us (11%)
  between operations  0.69 us (2%)
  other arithmetic  0.61 us (1%)
    pallas_call x1, Pallas kernels, body(): pl.pallas_call(functools.partial(kernel, nx, ny), out_shape=[jax.ShapeDty...  35.8 us
    unnamed x12, local copies, waits for them, and re-layouts  3.56 us

profile of v3, /device:TPU:0, one launch (start us, length us, event | category | flops | bytes accessed | tf_op | source)
XLA Modules:
  0.0 41.6 jit_solution(11796310970249544755)
XLA Ops:
  0.6 0.0 copy-start.3
  0.6 0.8 %stack_reshape.3 = f32[1,64]{1,0:T(1,128)S(1)} reshape(f32[4,4,4]{2,1,0:T(4,128)} %param.18) | data formatting | bytes 512 | tf_op jit(solution)/shard_map/stack;reshape | solution.py:422
  1.4 0.0 copy-done.3
  1.5 0.1 convert_element_type.16
  1.5 0.6 %select_maximum_fusion.ties_ref = f32[8,128]{1,0:T(8,128)} fusion(f32[1,64]{1,0:T(1,128)S(1)} %stack_reshape.3, f32[1,64]{1,0:T(1,128)S(1)} %convert_element_type.16), kind=kLoop, calls=%fused_computation | loop fusion | flops 8192 | bytes 4608 | tf_op jit(solution)/shard_map/stack | solution.py:422
  2.2 35.8 %hydro.1 = (f32[3,4,4,256]{3,2,1,0:T(4,128)}, f32[4,4,256]{2,1,0:T(4,128)}, f32[3,4096]{1,0:T(4,128)}, f32[3,4096]{1,0:T(4,128)}) custom-call(f32[3,4,4,256]{3,2,1,0:T(4,128)} %pos_ref.1, f32[3,4,4,256]{3,2,1,0:T(4,128)} %vel_ref.1, f32[4,4,256]{2,1,0:T(4,128)} %rho_ref.1, s32[4,4]{1,0:T(4,128)} %fill_ref.1, s32[2,86]{1,0:T(2,128)} %bitcast.2, ...), custom_call_target="tpu_custom_call" | custom-call | tf_op jit(solution)/shard_map/hydro/pallas_call | solution.py:427
  38.0 0.0 copy-start.2
  38.0 0.0 copy-start.1
  38.0 1.5 %copy.19 = f32[3,4,4,256]{3,2,1,0:T(4,128)} copy(f32[3,4,4,256]{3,2,1,0:T(4,128)} %get-tuple-element.8) | data formatting | bytes 98304
  39.5 0.0 copy-done.2
  39.5 0.6 %copy.20 = f32[4,4,256]{2,1,0:T(4,128)} copy(f32[4,4,256]{2,1,0:T(4,128)S(1)} %copy-done.2) | data formatting | bytes 32768
  40.1 0.0 copy-done.1
  40.1 0.0 copy-start
  40.1 0.6 %copy.21 = f32[3,4096]{1,0:T(4,128)} copy(f32[3,4096]{1,0:T(4,128)S(1)} %copy-done.1) | data formatting | bytes 98304
  40.7 0.2 copy-done
  40.9 0.6 %copy.22 = f32[3,4096]{1,0:T(4,128)} copy(f32[3,4096]{1,0:T(4,128)S(1)} %copy-done) | data formatting | bytes 98304
  (1 shorter events, 0.0 us)
Async XLA Ops:
  0.6 0.8 %copy-start.3 = (s32[4,4,4]{2,1,0:T(4,128)S(1)}, s32[4,4,4]{2,1,0:T(4,128)}, u32[]{:S(2)}) copy-start(s32[4,4,4]{2,1,0:T(4,128)} %param.17) | copy-start | bytes 772
  38.0 1.5 %copy-start.2 = (f32[4,4,256]{2,1,0:T(4,128)S(1)}, f32[4,4,256]{2,1,0:T(4,128)}, u32[]{:S(2)}) copy-start(f32[4,4,256]{2,1,0:T(4,128)} %get-tuple-element.9) | copy-start | bytes 49156
  38.0 2.1 %copy-start.1 = (f32[3,4096]{1,0:T(4,128)S(1)}, f32[3,4096]{1,0:T(4,128)}, u32[]{:S(2)}) copy-start(f32[3,4096]{1,0:T(4,128)} %get-tuple-element.10) | copy-start | bytes 147460
  40.1 0.9 %copy-start = (f32[3,4096]{1,0:T(4,128)S(1)}, f32[3,4096]{1,0:T(4,128)}, u32[]{:S(2)}) copy-start(f32[3,4096]{1,0:T(4,128)} %get-tuple-element.11) | copy-start | bytes 147460
